TPU v7x, 32 devices: a whole 2x2x4 slice. The times are simulated.
32 devices in a mesh: dp: 2 (over y), ep: 16 (over z, x, core).
Axes of the slice: x: 2, y: 2, z: 4, core: 2. Of those that a mesh axis runs over, the one named last changes fastest.
Arguments:
- expert_ids: int32 [2, 256, 8], P('dp', 'ep'), may hold values from 0 to 15, all different within a row; in each aligned block of 16 rows (0 to 15, 16 to 31, ..., all dimensions but the last counted through in order) at most 16 rows name the same one
- route_weights: float32 [2, 256, 8], P('dp', 'ep'), may hold values from 0.03 to 0.4
- saved_rows: bfloat16 [2, 16, 256, 2048], P('dp', 'ep'), may hold values from -6 to 6
- saved_gate_up: bfloat16 [2, 16, 256, 1536], P('dp', 'ep'), may hold values from -6 to 6
- hidden_grad: bfloat16 [2, 16, 256, 768], P('dp', 'ep'), may hold values from -6 to 6
- gate_up_weight: bfloat16 [16, 2048, 1536], P('ep'), may hold values from -0.125 to 0.125
Outputs:
- input_grad: bfloat16 [2, 256, 2048], P('dp', 'ep')
- weight_grad: float32 [2048, 16, 1536], P('dp', 'ep')
Inputs may be any that keep to these rules, and one draw needn't show every extreme that they name: `expert_ids`: each token names 8 different experts; among the tokens of one device no expert is named more than 16 times, a bound that some block reaches.
All inputs are finite; a program needn't handle non-finite values.
Results may differ from a plain program's by a relative error of at most 0.017.
Values may be sent and summed in bfloat16 or wider, within the bound.
A program may use at most 64 MiB of HBM per device.

v0:
```python
import functools

import jax
import jax.numpy as jnp
from jax import lax
from jax.experimental import pallas as pl
from jax.experimental.pallas import tpu as pltpu
from jax.sharding import PartitionSpec as P

F32 = jnp.float32
BF16 = jnp.bfloat16
LANES = 128
PIECES = 2
VMEM_LIMIT = 56 * 2**20


def reversed_bits(value, bits):
    out = value * 0
    for b in range(bits):
        out = out * 2 + (value // 2**b) % 2
    return out


def exchange_kernel(
    n_dp, n_ep, stages, ids_ref, route_ref, rows_hbm, gate_up_hbm, hidden_hbm, weight_hbm,
    rows_all, grads_all, token_out,
    route_send, route_recv, route_col, gate_up, hidden, weight, grads, mixed, total,
    load_sem, own_sem, route_ssem, route_rsem, rows_ssem, rows_rsem, grads_ssem, grads_rsem,
    half_ssem, half_rsem, *halves,
):
    sends, recvs = halves[:stages], halves[stages:]
    my_dp = lax.axis_index("dp")
    my_ep = lax.axis_index("ep")
    tokens = ids_ref.shape[1]
    slots, width2 = grads.shape
    width = width2 // 2
    model = weight.shape[0]
    share = model // n_dp
    cap = slots // n_ep
    all_tokens = n_ep * tokens
    piece = model // PIECES

    loads = [
        pltpu.make_async_copy(gate_up_hbm.at[0, 0], gate_up, load_sem.at[0]),
        pltpu.make_async_copy(hidden_hbm.at[0, 0], hidden, load_sem.at[1]),
        pltpu.make_async_copy(weight_hbm.at[0], weight, load_sem.at[2]),
    ]
    for load in loads:
        load.start()

    barrier = pltpu.get_barrier_semaphore()
    for k in range(1, n_ep):
        pl.semaphore_signal(barrier, inc=1, device_id={"ep": lax.rem(my_ep + k, n_ep)}, device_id_type=pl.DeviceIdType.MESH)
    for k in range(1, n_dp):
        pl.semaphore_signal(barrier, inc=1, device_id={"dp": lax.rem(my_dp + k, n_dp)}, device_id_type=pl.DeviceIdType.MESH)

    route_send[...] = jnp.zeros_like(route_send)
    ids = ids_ref[...]
    route = route_ref[...]
    for x in range(n_ep):
        route_send[x, :, 0:tokens] = jnp.sum(jnp.where(ids == x, route, 0.0), axis=0, keepdims=True)
    pl.semaphore_wait(barrier, n_ep - 1 + n_dp - 1)

    my_place = reversed_bits(my_ep, stages)
    route_copies = []
    for k in range(1, n_ep):
        to = lax.rem(my_ep + k, n_ep)
        route_copies.append(pltpu.make_async_remote_copy(
            src_ref=route_send.at[to], dst_ref=route_recv.at[my_place],
            send_sem=route_ssem.at[k], recv_sem=route_rsem.at[k],
            device_id={"ep": to}, device_id_type=pl.DeviceIdType.MESH))
    for copy in route_copies:
        copy.start()
    rows_copies = []
    for k in range(1, n_dp):
        to = lax.rem(my_dp + k, n_dp)
        rows_copies.append(pltpu.make_async_remote_copy(
            src_ref=rows_hbm.at[0, 0, :, pl.ds(pl.multiple_of(to * share, LANES), share)],
            dst_ref=rows_all.at[my_dp],
            send_sem=rows_ssem.at[k], recv_sem=rows_rsem.at[k],
            device_id={"dp": to}, device_id_type=pl.DeviceIdType.MESH))
    for copy in rows_copies:
        copy.start()
    own_rows = pltpu.make_async_copy(
        rows_hbm.at[0, 0, :, pl.ds(pl.multiple_of(my_dp * share, LANES), share)], rows_all.at[my_dp], own_sem.at[0])
    own_rows.start()
    own_route = pltpu.make_async_copy(route_send.at[my_ep], route_recv.at[my_place], own_sem.at[1])
    own_route.start()
    own_route.wait()
    for copy in route_copies:
        copy.wait()

    diagonal = lax.broadcasted_iota(jnp.int32, (tokens, LANES), 0) == lax.broadcasted_iota(jnp.int32, (tokens, LANES), 1)
    for p in range(n_ep):
        spread = jnp.broadcast_to(route_recv[p], (tokens, LANES))
        route_col[p * tokens:(p + 1) * tokens, :] = jnp.broadcast_to(
            jnp.sum(jnp.where(diagonal, spread, 0.0), axis=1, keepdims=True), (tokens, LANES))
    chosen = jnp.where(route_col[...] > 0.0, 1.0, 0.0).astype(BF16)

    slot = lax.broadcasted_iota(jnp.int32, (slots, all_tokens), 0)
    token = lax.broadcasted_iota(jnp.int32, (slots, all_tokens), 1)
    same = slot // cap == reversed_bits(token // tokens, stages)
    counts = jnp.dot(jnp.where(same, 1.0, 0.0).astype(BF16), chosen, preferred_element_type=F32)
    within = lax.broadcasted_iota(jnp.int32, (slots, LANES), 0) % cap
    live = (within.astype(F32) < counts)[:, 0:1]

    for load in loads[:2]:
        load.wait()
    strip = LANES * 2
    for c in range(width // strip):
        cols = slice(c * strip, (c + 1) * strip)
        upper = slice(width + c * strip, width + (c + 1) * strip)
        g = gate_up[:, cols].astype(F32)
        u = gate_up[:, upper].astype(F32)
        h = hidden[:, cols].astype(F32)
        q = jax.nn.sigmoid(g)
        hq = h * q
        grads[:, cols] = jnp.where(live, hq * u * (1.0 + g * (1.0 - q)), 0.0).astype(BF16)
        grads[:, upper] = jnp.where(live, hq * g, 0.0).astype(BF16)
    grads_copies = []
    for k in range(1, n_dp):
        grads_copies.append(pltpu.make_async_remote_copy(
            src_ref=grads, dst_ref=grads_all.at[my_dp],
            send_sem=grads_ssem.at[k], recv_sem=grads_rsem.at[k],
            device_id={"dp": lax.rem(my_dp + k, n_dp)}, device_id_type=pl.DeviceIdType.MESH))
    for copy in grads_copies:
        copy.start()
    own_grads = pltpu.make_async_copy(grads, grads_all.at[my_dp], own_sem.at[2])
    own_grads.start()

    t0 = lax.broadcasted_iota(jnp.int32, (all_tokens, all_tokens), 0)
    t1 = lax.broadcasted_iota(jnp.int32, (all_tokens, all_tokens), 1)
    earlier = (t0 // tokens == t1 // tokens) & (t1 < t0)
    rank = jnp.dot(jnp.where(earlier, 1.0, 0.0).astype(BF16), chosen, preferred_element_type=F32)[:, 0:1]
    token_row = lax.broadcasted_iota(jnp.int32, (all_tokens, slots), 0)
    slot_col = lax.broadcasted_iota(jnp.int32, (all_tokens, slots), 1)
    offset = (slot_col - reversed_bits(token_row // tokens, stages) * cap).astype(F32)
    picks = jnp.where(offset == rank, 1.0, 0.0).astype(BF16)
    factor = route_col[:, 0:1]
    for c in range(width2 // strip):
        cols = slice(c * strip, (c + 1) * strip)
        moved = jnp.dot(picks, grads[:, cols], preferred_element_type=F32)
        mixed[:, cols] = (moved * factor).astype(BF16)

    loads[2].wait()
    half = all_tokens // 2
    step_cols = 256

    def product(which, part, put):
        left = mixed[pl.ds(pl.multiple_of(which * half, 16), half), :]
        for c in range(piece // step_cols):
            right = weight[part * piece + c * step_cols:part * piece + (c + 1) * step_cols, :]
            put(slice(c * step_cols, (c + 1) * step_cols),
                lax.dot_general(left, right, (((1,), (1,)), ((), ())), preferred_element_type=F32))

    def copy_of(stage, part):
        bit = (my_ep // 2**stage) % 2
        return pltpu.make_async_remote_copy(
            src_ref=sends[stage].at[part], dst_ref=recvs[stage].at[part],
            send_sem=half_ssem.at[stage, part], recv_sem=half_rsem.at[stage, part],
            device_id={"ep": my_ep + (1 - 2 * bit) * 2**stage}, device_id_type=pl.DeviceIdType.MESH)

    copies = {(s, part): copy_of(s, part) for s in range(stages) for part in range(PIECES)}
    first = my_ep % 2
    for part in range(PIECES):
        def put_send(cols, value, part=part):
            sends[0][part, :, cols] = value.astype(BF16)
        product(1 - first, part, put_send)
        copies[0, part].start()
    for part in range(PIECES):
        def put_keep(cols, value, part=part):
            total[part, :, cols] = value
        product(first, part, put_keep)

    base = my_ep * 0
    for s in range(1, stages + 1):
        if s < stages:
            size = all_tokens // 2**(s + 1)
            bit = (my_ep // 2**s) % 2
            give = pl.multiple_of((1 - bit) * size, 16)
            keep = pl.multiple_of(bit * size, 16)
            give_at = pl.multiple_of(base + (1 - bit) * size, 16)
            keep_at = pl.multiple_of(base + bit * size, 16)
            for part in range(PIECES):
                copies[s - 1, part].wait_recv()
                sends[s][part] = (total[part, pl.ds(give_at, size), :]
                                  + recvs[s - 1][part, pl.ds(give, size), :].astype(F32)).astype(BF16)
                copies[s, part].start()
                total[part, pl.ds(keep_at, size), :] = (
                    total[part, pl.ds(keep_at, size), :] + recvs[s - 1][part, pl.ds(keep, size), :].astype(F32))
            base = base + bit * size
        else:
            at = pl.multiple_of(base, 16)
            for part in range(PIECES):
                copies[s - 1, part].wait_recv()
                token_out[:, part * piece:(part + 1) * piece] = (
                    total[part, pl.ds(at, tokens), :] + recvs[s - 1][part].astype(F32)).astype(BF16)
    for copy in copies.values():
        copy.wait_send()
    own_rows.wait()
    own_grads.wait()
    for copy in rows_copies + grads_copies:
        copy.wait()


def weight_kernel(scale, rows_ref, grads_ref, token_ref, out_ref, token_out):
    @pl.when(pl.program_id(0) == 0)
    def _():
        token_out[...] = token_ref[...]

    n_dp, slots, block = rows_ref.shape
    width2 = grads_ref.shape[2]
    rows = rows_ref[...].reshape(n_dp * slots, block)
    strips = width2 // LANES
    chunk = 2 * LANES
    for c in range(width2 // chunk):
        grads = grads_ref[:, :, c * chunk:(c + 1) * chunk].reshape(n_dp * slots, chunk)
        value = lax.dot_general(rows, grads, (((0,), (0,)), ((), ())), preferred_element_type=F32) * scale
        for j in range(chunk // LANES):
            out_ref[pl.ds(c * (chunk // LANES) + j, block, stride=strips), :] = value[:, j * LANES:(j + 1) * LANES]


def shards(expert_ids, route_weights, saved_rows, saved_gate_up, hidden_grad, gate_up_weight):
    n_ep = lax.axis_size("ep")
    n_dp = lax.axis_size("dp")
    tokens, top = expert_ids.shape[1:]
    slots, model = saved_rows.shape[2:]
    width = hidden_grad.shape[3]
    width2 = 2 * width
    share = model // n_dp
    all_tokens = n_ep * tokens
    stages = n_ep.bit_length() - 1
    piece = model // PIECES
    vmem = pl.BlockSpec(memory_space=pltpu.VMEM)
    hbm = pl.BlockSpec(memory_space=pl.ANY)
    dma = pltpu.SemaphoreType.DMA
    parts = [pltpu.VMEM((PIECES, all_tokens // 2**(s + 1), piece), BF16) for s in range(stages)]
    rows_all, grads_all, token_grad = pl.pallas_call(
        functools.partial(exchange_kernel, n_dp, n_ep, stages),
        out_shape=(
            jax.ShapeDtypeStruct((n_dp, slots, share), BF16),
            jax.ShapeDtypeStruct((n_dp, slots, width2), BF16),
            jax.ShapeDtypeStruct((tokens, model), BF16),
        ),
        in_specs=[vmem, vmem, hbm, hbm, hbm, hbm],
        out_specs=(hbm, hbm, vmem),
        scratch_shapes=[
            pltpu.VMEM((n_ep, 1, LANES), F32),
            pltpu.VMEM((n_ep, 1, LANES), F32),
            pltpu.VMEM((all_tokens, LANES), F32),
            pltpu.VMEM((slots, width2), BF16),
            pltpu.VMEM((slots, width), BF16),
            pltpu.VMEM((model, width2), BF16),
            pltpu.VMEM((slots, width2), BF16),
            pltpu.VMEM((all_tokens, width2), BF16),
            pltpu.VMEM((PIECES, all_tokens // 2, piece), F32),
            dma((3,)), dma((3,)),
            dma((n_ep,)), dma((n_ep,)),
            dma((n_dp,)), dma((n_dp,)),
            dma((n_dp,)), dma((n_dp,)),
            dma((stages, PIECES)), dma((stages, PIECES)),
            *parts, *parts,
        ],
        compiler_params=pltpu.CompilerParams(
            collective_id=0, has_side_effects=True, vmem_limit_bytes=VMEM_LIMIT),
    )(
        expert_ids.reshape(tokens, top).T, route_weights.reshape(tokens, top).T,
        saved_rows, saved_gate_up, hidden_grad, gate_up_weight,
    )
    block = min(share, 128)
    strips = width2 // LANES
    flat, token_grad = pl.pallas_call(
        functools.partial(weight_kernel, 1.0 / n_dp),
        grid=(share // block,),
        out_shape=(
            jax.ShapeDtypeStruct((share * strips, LANES), F32),
            jax.ShapeDtypeStruct((tokens, model), BF16),
        ),
        in_specs=[
            pl.BlockSpec((n_dp, slots, block), lambda i: (0, 0, i)),
            pl.BlockSpec((n_dp, slots, width2), lambda i: (0, 0, 0)),
            pl.BlockSpec((tokens, model), lambda i: (0, 0)),
        ],
        out_specs=(
            pl.BlockSpec((block * strips, LANES), lambda i: (i, 0)),
            pl.BlockSpec((tokens, model), lambda i: (0, 0)),
        ),
        compiler_params=pltpu.CompilerParams(vmem_limit_bytes=VMEM_LIMIT),
    )(rows_all, grads_all, token_grad)
    return token_grad.reshape(1, tokens, model), flat.reshape(share, 1, width2)


def solution(mesh):
    in_specs = (
        P("dp", "ep", None),
        P("dp", "ep", None),
        P("dp", "ep", None, None),
        P("dp", "ep", None, None),
        P("dp", "ep", None, None),
        P("ep", None, None),
    )
    out_specs = (P("dp", "ep", None), P("dp", "ep", None))
    return jax.shard_map(shards, mesh=mesh, in_specs=in_specs, out_specs=out_specs, check_vma=False)
```

profile of v0, /device:TPU:0, one launch (start us, length us, event | category | flops | bytes accessed | tf_op | source)
XLA Modules:
  0.0 47.6 jit_solution(6937886485524834204)
XLA Ops:
  0.6 38.8 %shard_map.77 = (bf16[2,256,1024]{2,1,0:T(8,128)(2,1)}, bf16[2,256,1536]{2,1,0:T(8,128)(2,1)}, bf16[16,2048]{1,0:T(8,128)(2,1)}) custom-call(s32[8,16]{1,0:T(8,128)} %bitcast.8, f32[8,16]{1,0:T(8,128)} %bitcast.9, bf16[1,1,256,2048]{3,2,1,0:T(8,128)(2,1)} %rows_hbm.1, bf16[1,1,256,1536]{3,2,1,0:T(8,128)(2,1)} %gate_up_hbm.1, ...), custom_call_target="tpu_custom_call" | custom-call | tf_op jit(solution)/shard_map/pallas_call | solution.py:238
  39.4 8.2 %shard_map.78 = (f32[12288,128]{1,0:T(8,128)}, bf16[16,2048]{1,0:T(8,128)(2,1)}) custom-call(bf16[2,256,1024]{2,1,0:T(8,128)(2,1)} %get-tuple-element.7.rows_ref, bf16[2,256,1536]{2,1,0:T(8,128)(2,1)} %get-tuple-element.8.grads_ref, bf16[16,2048]{1,0:T(8,128)(2,1)} %get-tuple-element.9.token_ref), custom_call_target="tpu_custom_call" | custom-call | tf_op jit(solution)/shard_map/pallas_call | solution.py:272
where the time goes:
time: 47.9 us; the launch traced here: 47.6 us
  Pallas kernels  47 us (98%)
  between operations  0.64 us (1%)
    pallas_call x1, Pallas kernels, shards(): pl.pallas_call(functools.partial(exchange_kernel, n_dp, n_ep, stages), ou...  38.8 us
    pallas_call x1, Pallas kernels, shards(): pl.pallas_call(functools.partial(weight_kernel, 1.0 / n_dp), grid=(share...  8.18 us

commit v1 on v0

--- a/solution.py
+++ b/solution.py
@@ -24,11 +24,11 @@
 def exchange_kernel(
     n_dp, n_ep, stages, ids_ref, route_ref, rows_hbm, gate_up_hbm, hidden_hbm, weight_hbm,
     rows_all, grads_all, token_out,
-    route_send, route_recv, route_col, gate_up, hidden, weight, grads, mixed, total,
+    route_rows, route_col, gate_up, hidden, weight, grads, mixed, total,
     load_sem, own_sem, route_ssem, route_rsem, rows_ssem, rows_rsem, grads_ssem, grads_rsem,
     half_ssem, half_rsem, *halves,
 ):
-    sends, recvs = halves[:stages], halves[stages:]
+    sends, recvs, route_sends, route_recvs = (halves[i * stages:(i + 1) * stages] for i in range(4))
     my_dp = lax.axis_index("dp")
     my_ep = lax.axis_index("ep")
     tokens = ids_ref.shape[1]
@@ -48,29 +48,21 @@
     for load in loads:
         load.start()
 
+    bits = [(my_ep // 2**stage) % 2 for stage in range(stages)]
+    partners = [my_ep + (1 - 2 * bits[stage]) * 2**stage for stage in range(stages)]
     barrier = pltpu.get_barrier_semaphore()
-    for k in range(1, n_ep):
-        pl.semaphore_signal(barrier, inc=1, device_id={"ep": lax.rem(my_ep + k, n_ep)}, device_id_type=pl.DeviceIdType.MESH)
     for k in range(1, n_dp):
         pl.semaphore_signal(barrier, inc=1, device_id={"dp": lax.rem(my_dp + k, n_dp)}, device_id_type=pl.DeviceIdType.MESH)
-
-    route_send[...] = jnp.zeros_like(route_send)
+    for partner in partners:
+        pl.semaphore_signal(barrier, inc=1, device_id={"ep": partner}, device_id_type=pl.DeviceIdType.MESH)
+
+    route_rows[...] = jnp.zeros_like(route_rows)
     ids = ids_ref[...]
     route = route_ref[...]
     for x in range(n_ep):
-        route_send[x, :, 0:tokens] = jnp.sum(jnp.where(ids == x, route, 0.0), axis=0, keepdims=True)
-    pl.semaphore_wait(barrier, n_ep - 1 + n_dp - 1)
-
-    my_place = reversed_bits(my_ep, stages)
-    route_copies = []
-    for k in range(1, n_ep):
-        to = lax.rem(my_ep + k, n_ep)
-        route_copies.append(pltpu.make_async_remote_copy(
-            src_ref=route_send.at[to], dst_ref=route_recv.at[my_place],
-            send_sem=route_ssem.at[k], recv_sem=route_rsem.at[k],
-            device_id={"ep": to}, device_id_type=pl.DeviceIdType.MESH))
-    for copy in route_copies:
-        copy.start()
+        route_rows[x, :, 0:tokens] = jnp.sum(jnp.where(ids == x, route, 0.0), axis=0, keepdims=True)
+    pl.semaphore_wait(barrier, n_dp - 1 + stages)
+
     rows_copies = []
     for k in range(1, n_dp):
         to = lax.rem(my_dp + k, n_dp)
@@ -81,18 +73,57 @@
             device_id={"dp": to}, device_id_type=pl.DeviceIdType.MESH))
     for copy in rows_copies:
         copy.start()
+
+    route_copies = []
+
+    def entry(stage, i):
+        return i // 2**stage * 2**(stage + 1) + (1 - bits[stage]) * 2**stage + i % 2**stage
+
+    def route_start(stage):
+        for i in range(n_ep // 2):
+            route_sends[stage][i] = route_rows[entry(stage, i)]
+        copy = pltpu.make_async_remote_copy(
+            src_ref=route_sends[stage], dst_ref=route_recvs[stage],
+            send_sem=route_ssem.at[stage], recv_sem=route_rsem.at[stage],
+            device_id={"ep": partners[stage]}, device_id_type=pl.DeviceIdType.MESH)
+        copy.start()
+        route_copies.append(copy)
+
+    def route_finish(stage):
+        route_copies[stage].wait()
+        for i in range(n_ep // 2):
+            route_rows[entry(stage, i)] = route_recvs[stage][i]
+
+    route_start(0)
     own_rows = pltpu.make_async_copy(
         rows_hbm.at[0, 0, :, pl.ds(pl.multiple_of(my_dp * share, LANES), share)], rows_all.at[my_dp], own_sem.at[0])
     own_rows.start()
-    own_route = pltpu.make_async_copy(route_send.at[my_ep], route_recv.at[my_place], own_sem.at[1])
-    own_route.start()
-    own_route.wait()
-    for copy in route_copies:
-        copy.wait()
+    for load in loads[:2]:
+        load.wait()
+    strip = LANES * 2
+    strips = width // strip
+
+    def slot_strips(first, last):
+        for c in range(first, last):
+            cols = slice(c * strip, (c + 1) * strip)
+            upper = slice(width + c * strip, width + (c + 1) * strip)
+            g = gate_up[:, cols].astype(F32)
+            u = gate_up[:, upper].astype(F32)
+            h = hidden[:, cols].astype(F32)
+            q = jax.nn.sigmoid(g)
+            hq = h * q
+            grads[:, cols] = (hq * u * (1.0 + g * (1.0 - q))).astype(BF16)
+            grads[:, upper] = (hq * g).astype(BF16)
+
+    for stage in range(stages):
+        slot_strips(strips * stage // stages, strips * (stage + 1) // stages)
+        route_finish(stage)
+        if stage + 1 < stages:
+            route_start(stage + 1)
 
     diagonal = lax.broadcasted_iota(jnp.int32, (tokens, LANES), 0) == lax.broadcasted_iota(jnp.int32, (tokens, LANES), 1)
     for p in range(n_ep):
-        spread = jnp.broadcast_to(route_recv[p], (tokens, LANES))
+        spread = jnp.broadcast_to(route_rows[reversed_bits(p, stages)], (tokens, LANES))
         route_col[p * tokens:(p + 1) * tokens, :] = jnp.broadcast_to(
             jnp.sum(jnp.where(diagonal, spread, 0.0), axis=1, keepdims=True), (tokens, LANES))
     chosen = jnp.where(route_col[...] > 0.0, 1.0, 0.0).astype(BF16)
@@ -104,19 +135,9 @@
     within = lax.broadcasted_iota(jnp.int32, (slots, LANES), 0) % cap
     live = (within.astype(F32) < counts)[:, 0:1]
 
-    for load in loads[:2]:
-        load.wait()
-    strip = LANES * 2
-    for c in range(width // strip):
+    for c in range(width2 // strip):
         cols = slice(c * strip, (c + 1) * strip)
-        upper = slice(width + c * strip, width + (c + 1) * strip)
-        g = gate_up[:, cols].astype(F32)
-        u = gate_up[:, upper].astype(F32)
-        h = hidden[:, cols].astype(F32)
-        q = jax.nn.sigmoid(g)
-        hq = h * q
-        grads[:, cols] = jnp.where(live, hq * u * (1.0 + g * (1.0 - q)), 0.0).astype(BF16)
-        grads[:, upper] = jnp.where(live, hq * g, 0.0).astype(BF16)
+        grads[:, cols] = jnp.where(live, grads[:, cols].astype(F32), 0.0).astype(BF16)
     grads_copies = []
     for k in range(1, n_dp):
         grads_copies.append(pltpu.make_async_remote_copy(
@@ -154,11 +175,10 @@
                 lax.dot_general(left, right, (((1,), (1,)), ((), ())), preferred_element_type=F32))
 
     def copy_of(stage, part):
-        bit = (my_ep // 2**stage) % 2
         return pltpu.make_async_remote_copy(
             src_ref=sends[stage].at[part], dst_ref=recvs[stage].at[part],
             send_sem=half_ssem.at[stage, part], recv_sem=half_rsem.at[stage, part],
-            device_id={"ep": my_ep + (1 - 2 * bit) * 2**stage}, device_id_type=pl.DeviceIdType.MESH)
+            device_id={"ep": partners[stage]}, device_id_type=pl.DeviceIdType.MESH)
 
     copies = {(s, part): copy_of(s, part) for s in range(stages) for part in range(PIECES)}
     first = my_ep % 2
@@ -176,7 +196,7 @@
     for s in range(1, stages + 1):
         if s < stages:
             size = all_tokens // 2**(s + 1)
-            bit = (my_ep // 2**s) % 2
+            bit = bits[s]
             give = pl.multiple_of((1 - bit) * size, 16)
             keep = pl.multiple_of(bit * size, 16)
             give_at = pl.multiple_of(base + (1 - bit) * size, 16)
@@ -235,6 +255,7 @@
     hbm = pl.BlockSpec(memory_space=pl.ANY)
     dma = pltpu.SemaphoreType.DMA
     parts = [pltpu.VMEM((PIECES, all_tokens // 2**(s + 1), piece), BF16) for s in range(stages)]
+    routes = [pltpu.VMEM((n_ep // 2, 1, LANES), F32)] * stages
     rows_all, grads_all, token_grad = pl.pallas_call(
         functools.partial(exchange_kernel, n_dp, n_ep, stages),
         out_shape=(
@@ -246,7 +267,6 @@
         out_specs=(hbm, hbm, vmem),
         scratch_shapes=[
             pltpu.VMEM((n_ep, 1, LANES), F32),
-            pltpu.VMEM((n_ep, 1, LANES), F32),
             pltpu.VMEM((all_tokens, LANES), F32),
             pltpu.VMEM((slots, width2), BF16),
             pltpu.VMEM((slots, width), BF16),
@@ -255,11 +275,11 @@
             pltpu.VMEM((all_tokens, width2), BF16),
             pltpu.VMEM((PIECES, all_tokens // 2, piece), F32),
             dma((3,)), dma((3,)),
-            dma((n_ep,)), dma((n_ep,)),
+            dma((stages,)), dma((stages,)),
             dma((n_dp,)), dma((n_dp,)),
             dma((n_dp,)), dma((n_dp,)),
             dma((stages, PIECES)), dma((stages, PIECES)),
-            *parts, *parts,
+            *parts, *parts, *routes, *routes,
         ],
         compiler_params=pltpu.CompilerParams(
             collective_id=0, has_side_effects=True, vmem_limit_bytes=VMEM_LIMIT),
@@ -267,7 +287,7 @@
         expert_ids.reshape(tokens, top).T, route_weights.reshape(tokens, top).T,
         saved_rows, saved_gate_up, hidden_grad, gate_up_weight,
     )
-    block = min(share, 128)
+    block = min(share, 512)
     strips = width2 // LANES
     flat, token_grad = pl.pallas_call(
         functools.partial(weight_kernel, 1.0 / n_dp),

time: 47.9 us -> 42.3 us (0.88)
  Pallas kernels: 47 us -> 41.4 us
    pallas_call x1, Pallas kernels: 8.18 us -> 5.36 us  [shards(): pl.pallas_call(functools.partial(weight_kernel, 1.0 / n_dp), grid=(share...]
    pallas_call x1, Pallas kernels: 38.8 us -> 36 us  [shards(): pl.pallas_call(functools.partial(exchange_kernel, n_dp, n_ep, stages), ou...]
where the time goes in v1:
time: 42.3 us; the launch traced here: 42 us
  Pallas kernels  41.4 us (98%)
  between operations  0.64 us (2%)
    pallas_call x1, Pallas kernels, shards(): pl.pallas_call(functools.partial(exchange_kernel, n_dp, n_ep, stages), ou...  36 us
    pallas_call x1, Pallas kernels, shards(): pl.pallas_call(functools.partial(weight_kernel, 1.0 / n_dp), grid=(share...  5.36 us

profile of v1, /device:TPU:0, one launch (start us, length us, event | category | flops | bytes accessed | tf_op | source)
XLA Modules:
  0.0 42.0 jit_solution(15194108374340383370)
XLA Ops:
  0.6 36.0 %shard_map.77 = (bf16[2,256,1024]{2,1,0:T(8,128)(2,1)}, bf16[2,256,1536]{2,1,0:T(8,128)(2,1)}, bf16[16,2048]{1,0:T(8,128)(2,1)}) custom-call(s32[8,16]{1,0:T(8,128)} %bitcast.8, f32[8,16]{1,0:T(8,128)} %bitcast.9, bf16[1,1,256,2048]{3,2,1,0:T(8,128)(2,1)} %rows_hbm.1, bf16[1,1,256,1536]{3,2,1,0:T(8,128)(2,1)} %gate_up_hbm.1, ...), custom_call_target="tpu_custom_call" | custom-call | tf_op jit(solution)/shard_map/pallas_call | solution.py:259
  36.7 5.4 %shard_map.78 = (f32[12288,128]{1,0:T(8,128)}, bf16[16,2048]{1,0:T(8,128)(2,1)}) custom-call(bf16[2,256,1024]{2,1,0:T(8,128)(2,1)} %get-tuple-element.7.rows_ref, bf16[2,256,1536]{2,1,0:T(8,128)(2,1)} %get-tuple-element.8.grads_ref, bf16[16,2048]{1,0:T(8,128)(2,1)} %get-tuple-element.9.token_ref), custom_call_target="tpu_custom_call" | custom-call | tf_op jit(solution)/shard_map/pallas_call | solution.py:292

commit v2 on v1

--- a/solution.py
+++ b/solution.py
@@ -11,7 +11,7 @@
 BF16 = jnp.bfloat16
 LANES = 128
 PIECES = 2
-VMEM_LIMIT = 56 * 2**20
+VMEM_LIMIT = 40 * 2**20
 
 
 def reversed_bits(value, bits):
@@ -223,21 +223,29 @@
         copy.wait()
 
 
-def weight_kernel(scale, rows_ref, grads_ref, token_ref, out_ref, token_out):
-    @pl.when(pl.program_id(0) == 0)
-    def _():
-        token_out[...] = token_ref[...]
-
-    n_dp, slots, block = rows_ref.shape
-    width2 = grads_ref.shape[2]
-    rows = rows_ref[...].reshape(n_dp * slots, block)
+def weight_kernel(scale, rows, grads, token_ref, out_hbm, token_out, out, out_sem):
+    n_dp, slots, share = rows.shape
+    width2 = grads.shape[2]
+    depth = n_dp * slots
     strips = width2 // LANES
     chunk = 2 * LANES
-    for c in range(width2 // chunk):
-        grads = grads_ref[:, :, c * chunk:(c + 1) * chunk].reshape(n_dp * slots, chunk)
-        value = lax.dot_general(rows, grads, (((0,), (0,)), ((), ())), preferred_element_type=F32) * scale
-        for j in range(chunk // LANES):
-            out_ref[pl.ds(c * (chunk // LANES) + j, block, stride=strips), :] = value[:, j * LANES:(j + 1) * LANES]
+    part = width2 // 1
+    block = min(share, 128)
+    token_out[...] = token_ref[...]
+    stores = []
+    for m in range(share // block):
+        left = rows[:, :, m * block:(m + 1) * block].reshape(depth, block)
+        for c in range(width2 // chunk):
+            right = grads[:, :, c * chunk:(c + 1) * chunk].reshape(depth, chunk)
+            value = lax.dot_general(left, right, (((0,), (0,)), ((), ())), preferred_element_type=F32) * scale
+            for j in range(chunk // LANES):
+                at = m * block * strips + c * (chunk // LANES) + j
+                out[pl.ds(at, block, stride=strips), :] = value[:, j * LANES:(j + 1) * LANES]
+        band = pl.ds(m * block * strips, block * strips)
+        stores.append(pltpu.make_async_copy(out.at[band], out_hbm.at[band], out_sem.at[m]))
+        stores[m].start()
+    for store in stores:
+        store.wait()
 
 
 def shards(expert_ids, route_weights, saved_rows, saved_gate_up, hidden_grad, gate_up_weight):
@@ -259,12 +267,12 @@
     rows_all, grads_all, token_grad = pl.pallas_call(
         functools.partial(exchange_kernel, n_dp, n_ep, stages),
         out_shape=(
-            jax.ShapeDtypeStruct((n_dp, slots, share), BF16),
-            jax.ShapeDtypeStruct((n_dp, slots, width2), BF16),
+            pltpu.VMEM((n_dp, slots, share), BF16),
+            pltpu.VMEM((n_dp, slots, width2), BF16),
             jax.ShapeDtypeStruct((tokens, model), BF16),
         ),
         in_specs=[vmem, vmem, hbm, hbm, hbm, hbm],
-        out_specs=(hbm, hbm, vmem),
+        out_specs=(vmem, vmem, vmem),
         scratch_shapes=[
             pltpu.VMEM((n_ep, 1, LANES), F32),
             pltpu.VMEM((all_tokens, LANES), F32),
@@ -285,26 +293,21 @@
             collective_id=0, has_side_effects=True, vmem_limit_bytes=VMEM_LIMIT),
     )(
         expert_ids.reshape(tokens, top).T, route_weights.reshape(tokens, top).T,
-        saved_rows, saved_gate_up, hidden_grad, gate_up_weight,
+        *(pltpu.with_memory_space_constraint(x, pltpu.HBM) for x in (saved_rows, saved_gate_up, hidden_grad, gate_up_weight)),
     )
-    block = min(share, 512)
     strips = width2 // LANES
     flat, token_grad = pl.pallas_call(
         functools.partial(weight_kernel, 1.0 / n_dp),
-        grid=(share // block,),
         out_shape=(
             jax.ShapeDtypeStruct((share * strips, LANES), F32),
             jax.ShapeDtypeStruct((tokens, model), BF16),
         ),
-        in_specs=[
-            pl.BlockSpec((n_dp, slots, block), lambda i: (0, 0, i)),
-            pl.BlockSpec((n_dp, slots, width2), lambda i: (0, 0, 0)),
-            pl.BlockSpec((tokens, model), lambda i: (0, 0)),
+        in_specs=[vmem, vmem, vmem],
+        out_specs=(hbm, vmem),
+        scratch_shapes=[
+            pltpu.VMEM((share * strips, LANES), F32),
+            dma((share // min(share, 128),)),
         ],
-        out_specs=(
-            pl.BlockSpec((block * strips, LANES), lambda i: (i, 0)),
-            pl.BlockSpec((tokens, model), lambda i: (0, 0)),
-        ),
         compiler_params=pltpu.CompilerParams(vmem_limit_bytes=VMEM_LIMIT),
     )(rows_all, grads_all, token_grad)
     return token_grad.reshape(1, tokens, model), flat.reshape(share, 1, width2)

time: 42.3 us -> 40.6 us (0.960)
  Pallas kernels: 41.4 us -> 38.4 us
  local copies, waits for them, and re-layouts: 0 us -> 1.37 us
    pallas_call x1, Pallas kernels: 5.36 us -> 3.78 us  [shards(): pl.pallas_call(functools.partial(weight_kernel, 1.0 / n_dp), out_shape=(j...]
    pallas_call x1, Pallas kernels: 36 us -> 34.6 us  [shards(): pl.pallas_call(functools.partial(exchange_kernel, n_dp, n_ep, stages), ou...]
    unnamed x0 -> x4, local copies, waits for them, and re-layouts: none -> 1.37 us
where the time goes in v2:
time: 40.6 us; the launch traced here: 40.4 us
  Pallas kernels  38.4 us (95%)
  local copies, waits for them, and re-layouts  1.37 us (3%)
  between operations  0.65 us (2%)
    pallas_call x1, Pallas kernels, shards(): pl.pallas_call(functools.partial(exchange_kernel, n_dp, n_ep, stages), ou...  34.6 us
    pallas_call x1, Pallas kernels, shards(): pl.pallas_call(functools.partial(weight_kernel, 1.0 / n_dp), out_shape=(j...  3.78 us
    unnamed x4, local copies, waits for them, and re-layouts  1.37 us

profile of v2, /device:TPU:0, one launch (start us, length us, event | category | flops | bytes accessed | tf_op | source)
XLA Modules:
  0.0 40.4 jit_solution(15418539598260393431)
XLA Ops:
  0.6 0.0 copy-start
  0.6 0.7 %copy-done = s32[1,16,8]{1,2,0:T(8,128)S(1)} copy-done((s32[1,16,8]{1,2,0:T(8,128)S(1)}, s32[1,16,8]{1,2,0:T(8,128)}, u32[]{:S(2)}) %copy-start) | copy-done | bytes 536
  1.3 0.0 copy-start.1
  1.3 0.7 %copy-done.1 = f32[1,16,8]{1,2,0:T(8,128)S(1)} copy-done((f32[1,16,8]{1,2,0:T(8,128)S(1)}, f32[1,16,8]{1,2,0:T(8,128)}, u32[]{:S(2)}) %copy-start.1) | copy-done | bytes 536
  2.0 34.6 %shard_map.77 = (bf16[2,256,1024]{2,1,0:T(8,128)(2,1)S(1)}, bf16[2,256,1536]{2,1,0:T(8,128)(2,1)S(1)}, bf16[16,2048]{1,0:T(8,128)(2,1)S(1)}) custom-call(s32[8,16]{1,0:T(8,128)S(1)} %bitcast.8, f32[8,16]{1,0:T(8,128)S(1)} %bitcast.9, bf16[1,1,256,2048]{3,2,1,0:T(8,128)(2,1)} %rows_hbm.1, bf16[1,1,256,1536]{3,2,1,0:T(8,128)(2,1)} %gate_up_hbm.1, ...), custom_call_target="tpu_custom_call" | custom-call | tf_op jit(solution)/shard_map/pallas_call | solution.py:267
  36.6 3.8 %shard_map.78 = (f32[12288,128]{1,0:T(8,128)}, bf16[16,2048]{1,0:T(8,128)(2,1)}) custom-call(bf16[2,256,1024]{2,1,0:T(8,128)(2,1)S(1)} %get-tuple-element.7.rows, bf16[2,256,1536]{2,1,0:T(8,128)(2,1)S(1)} %get-tuple-element.8.grads, bf16[16,2048]{1,0:T(8,128)(2,1)S(1)} %get-tuple-element.9.token_ref), custom_call_target="tpu_custom_call" | custom-call | tf_op jit(solution)/shard_map/pallas_call | solution.py:299
Async XLA Ops:
  0.6 0.7 %copy-start = (s32[1,16,8]{1,2,0:T(8,128)S(1)}, s32[1,16,8]{1,2,0:T(8,128)}, u32[]{:S(2)}) copy-start(s32[1,16,8]{1,2,0:T(8,128)} %param.6) | copy-start | bytes 1540
  1.3 0.7 %copy-start.1 = (f32[1,16,8]{1,2,0:T(8,128)S(1)}, f32[1,16,8]{1,2,0:T(8,128)}, u32[]{:S(2)}) copy-start(f32[1,16,8]{1,2,0:T(8,128)} %param.7) | copy-start | bytes 1540
